TPU v7x, 32 devices: a whole 2x2x4 slice. The times are simulated.
32 devices in a mesh: grp: 2 (over core), dp: 16 (over z, y, x).
Axes of the slice: x: 2, y: 2, z: 4, core: 2. Of those that a mesh axis runs over, the one named last changes fastest.
Arguments:
- tokens: bfloat16 [32768, 768], P(('grp', 'dp')), may hold values from -6 to 6
- out_grad: bfloat16 [32768, 768], P(('grp', 'dp')), may hold values from -6 to 6
- image_counts: int32 [32, 32], P(('grp', 'dp')), may hold values from 0 to 98, as said below
- group_of_device: int32 [32], P(('grp', 'dp')), may hold values from 0 to 2, as said below
- group_weight: int32 [3], replicated, may hold values from 1 to 4
- norm1_gain: bfloat16 [768], replicated, may hold values from 0.5 to 1.5
- norm1_bias: bfloat16 [768], replicated, may hold values from -4 to 4
- qkv_weight: bfloat16 [768, 2304], replicated, may hold values from -0.21875 to 0.21875
- qkv_bias: bfloat16 [2304], replicated, may hold values from -4 to 4
- proj_weight: bfloat16 [768, 768], replicated, may hold values from -0.875 to 0.875
- proj_bias: bfloat16 [768], replicated, may hold values from -4 to 4
- norm2_gain: bfloat16 [768], replicated, may hold values from 0.5 to 1.5
- norm2_bias: bfloat16 [768], replicated, may hold values from -4 to 4
- fc1_weight: bfloat16 [768, 3072], replicated, may hold values from -0.21875 to 0.21875
- fc1_bias: bfloat16 [3072], replicated, may hold values from -4 to 4
- fc2_weight: bfloat16 [3072, 768], replicated, may hold values from -0.109375 to 0.109375
- fc2_bias: bfloat16 [768], replicated, may hold values from -4 to 4
- first_moment: float32 [16, 442992], P('dp'), may hold values from -2.5 to 2.5
- second_moment: float32 [16, 442992], P('dp'), may hold values from 1e-05 to 0.001
Outputs:
- block_out: bfloat16 [32768, 768], P(('grp', 'dp'))
- input_grad: bfloat16 [32768, 768], P(('grp', 'dp'))
- weight_grads: float32 [16, 442992], P('dp')
- new_weights: bfloat16 [16, 442992], replicated
- new_first: float32 [16, 442992], P('dp')
- new_second: float32 [16, 442992], P('dp')
- fc2_bias_grad: float32 [768], P('dp')
Inputs may be any that keep to these rules, and one draw needn't show every extreme that they name: `group_of_device`: each of the 3 groups holds some devices: about a half, a third and a sixth of them. `image_counts`: in each device's row the live images come first, at least one, each with 30 to 98 visible patches, summing to at most 1024; the remaining slots are 0.
All inputs are finite; a program needn't handle non-finite values.
Results may differ from a plain program's by a relative error of at most 0.012.
Values may be sent and summed in bfloat16 or wider, within the bound.
No kernel may reach another device: no remote copies, remote signals or barrier semaphores. Data moves between devices by JAX's collectives and lax.ppermute only.
A program may use at most 320 MiB of HBM per device.

v0:
```python
import jax
import jax.numpy as jnp
from jax import lax
from jax.sharding import PartitionSpec as P

D = 768
HEADS = 12
HEAD_DIM = 64
NGROUPS = 3
beta_one = 0.9
beta_two = 0.999
adam_eps = 1e-08
decay_rate = 0.05
step_count = 10.0
learn_rate = 0.004 * 0.75**1
norm_eps = 1e-06
neg_fill = -1e30
decay_flags = (0.0, 0.0, 1.0, 0.0, 1.0, 0.0, 0.0, 0.0, 1.0, 0.0, 1.0, 0.0)


def layer_norm(values, gain, shift):
    center = values - jnp.mean(values, axis=-1, keepdims=True)
    spread = jnp.mean(center * center, axis=-1, keepdims=True)
    return center * lax.rsqrt(spread + norm_eps) * gain + shift


def gelu_tanh(values):
    return jax.nn.gelu(values, approximate=True)


def contract_rows(first_op, second_op):
    return lax.dot_general(
        first_op, second_op, (((0,), (0,)), ((), ())), preferred_element_type=jnp.float32
    )


def contract_cols(first_op, second_op):
    return lax.dot_general(
        first_op, second_op, (((1,), (1,)), ((), ())), preferred_element_type=jnp.float32
    )


def segment_info(counts_row, length):
    segment_ends = jnp.cumsum(counts_row)
    position = lax.iota(jnp.int32, length)
    segment = jnp.sum((position[:, None] >= segment_ends[None, :]).astype(jnp.int32), axis=1)
    return (segment, position < segment_ends[-1])


def score_block(query_part, key_rows, same_segment):
    raw = (
        jnp.einsum("qhd,khd->hqk", query_part, key_rows, preferred_element_type=jnp.float32) * 0.125
    )
    return jnp.where(same_segment[None], raw, neg_fill)


def on_device(
    tokens,
    out_grad,
    image_counts,
    group_of_device,
    group_weight,
    norm1_gain,
    norm1_bias,
    qkv_weight,
    qkv_bias,
    proj_weight,
    proj_bias,
    norm2_gain,
    norm2_bias,
    fc1_weight,
    fc1_bias,
    fc2_weight,
    fc2_bias,
    first_moment,
    second_moment,
):
    length = tokens.shape[0]
    segment, valid_rows = segment_info(image_counts[0], length)
    images = jnp.sum((image_counts[0] > 0).astype(jnp.int32))
    member = (group_of_device[0] == lax.iota(jnp.int32, NGROUPS)).astype(jnp.int32)
    totals = lax.psum(member * images, ("grp", "dp"))
    factor = jnp.sum(member * group_weight).astype(jnp.float32) / jnp.sum(member * totals).astype(
        jnp.float32
    )
    inputs = tokens.astype(jnp.float32)
    normed_one, norm_one_back = jax.vjp(
        layer_norm, inputs, norm1_gain.astype(jnp.float32), norm1_bias.astype(jnp.float32)
    )
    normed_one_low = normed_one.astype(jnp.bfloat16)
    projected = (
        jnp.dot(normed_one_low, qkv_weight, preferred_element_type=jnp.float32)
        + qkv_bias.astype(jnp.float32)
    ).astype(jnp.bfloat16)
    query_rows = projected[:, :D].reshape(length, HEADS, HEAD_DIM)
    key_rows = projected[:, D : 2 * D].reshape(length, HEADS, HEAD_DIM)
    value_rows = projected[:, 2 * D :].reshape(length, HEADS, HEAD_DIM)
    block_rows = min(512, length)
    offsets = list(range(0, length, block_rows))
    context_parts = []
    log_sums = []
    for offset in offsets:
        same_segment = segment[offset : offset + block_rows, None] == segment[None, :]
        scores = score_block(query_rows[offset : offset + block_rows], key_rows, same_segment)
        row_max = jnp.max(scores, axis=-1, keepdims=True)
        exponent = jnp.exp(scores - row_max)
        row_sum = jnp.sum(exponent, axis=-1, keepdims=True)
        attn_probs = exponent / row_sum
        log_sums.append(row_max + jnp.log(row_sum))
        context_parts.append(
            jnp.einsum(
                "hqk,khd->qhd",
                attn_probs.astype(jnp.bfloat16),
                value_rows,
                preferred_element_type=jnp.float32,
            )
        )
    context = jnp.concatenate(context_parts, axis=0).reshape(length, D).astype(jnp.bfloat16)
    middle = inputs + (
        jnp.dot(context, proj_weight, preferred_element_type=jnp.float32)
        + proj_bias.astype(jnp.float32)
    )
    normed_two, norm_two_back = jax.vjp(
        layer_norm, middle, norm2_gain.astype(jnp.float32), norm2_bias.astype(jnp.float32)
    )
    normed_two_low = normed_two.astype(jnp.bfloat16)
    hidden = jnp.dot(
        normed_two_low, fc1_weight, preferred_element_type=jnp.float32
    ) + fc1_bias.astype(jnp.float32)
    activated, gelu_back = jax.vjp(gelu_tanh, hidden)
    activated_low = activated.astype(jnp.bfloat16)
    block_out = (
        middle
        + (
            jnp.dot(activated_low, fc2_weight, preferred_element_type=jnp.float32)
            + fc2_bias.astype(jnp.float32)
        )
    ).astype(jnp.bfloat16)
    grad_out = out_grad.astype(jnp.float32) * valid_rows[:, None].astype(jnp.float32)
    grad_out_low = grad_out.astype(jnp.bfloat16)
    fc2_grad = contract_rows(activated_low, grad_out_low)
    fc2_bias_grad = jnp.sum(grad_out, axis=0)
    grad_hidden = gelu_back(contract_cols(grad_out_low, fc2_weight))[0].astype(jnp.bfloat16)
    fc1_grad = contract_rows(normed_two_low, grad_hidden)
    fc1_bias_grad = jnp.sum(grad_hidden.astype(jnp.float32), axis=0)
    grad_middle_norm, gain_two_grad, shift_two_grad = norm_two_back(
        contract_cols(grad_hidden, fc1_weight)
    )
    grad_middle = grad_out + grad_middle_norm
    grad_branch = grad_middle.astype(jnp.bfloat16)
    proj_grad = contract_rows(context, grad_branch)
    proj_bias_grad = jnp.sum(grad_branch.astype(jnp.float32), axis=0)
    grad_context = (
        contract_cols(grad_branch, proj_weight)
        .astype(jnp.bfloat16)
        .reshape(length, HEADS, HEAD_DIM)
    )
    grad_keys = jnp.zeros((length, HEADS, HEAD_DIM), jnp.float32)
    grad_values = jnp.zeros((length, HEADS, HEAD_DIM), jnp.float32)
    query_grads = []
    for piece_index, offset in enumerate(offsets):
        query_part = query_rows[offset : offset + block_rows]
        context_grad_part = grad_context[offset : offset + block_rows]
        same_segment = segment[offset : offset + block_rows, None] == segment[None, :]
        attn_probs = jnp.exp(
            score_block(query_part, key_rows, same_segment) - log_sums[piece_index]
        )
        grad_probs = jnp.einsum(
            "qhd,khd->hqk", context_grad_part, value_rows, preferred_element_type=jnp.float32
        )
        grad_scores = (
            attn_probs * (grad_probs - jnp.sum(attn_probs * grad_probs, axis=-1, keepdims=True))
        ).astype(jnp.bfloat16)
        query_grads.append(
            jnp.einsum("hqk,khd->qhd", grad_scores, key_rows, preferred_element_type=jnp.float32)
            * 0.125
        )
        grad_keys = (
            grad_keys
            + jnp.einsum(
                "hqk,qhd->khd", grad_scores, query_part, preferred_element_type=jnp.float32
            )
            * 0.125
        )
        grad_values = grad_values + jnp.einsum(
            "hqk,qhd->khd",
            attn_probs.astype(jnp.bfloat16),
            context_grad_part,
            preferred_element_type=jnp.float32,
        )
    grad_projected = jnp.concatenate(
        [
            jnp.concatenate(query_grads, axis=0).reshape(length, D),
            grad_keys.reshape(length, D),
            grad_values.reshape(length, D),
        ],
        axis=1,
    ).astype(jnp.bfloat16)
    qkv_grad = contract_rows(normed_one_low, grad_projected)
    qkv_bias_grad = jnp.sum(grad_projected.astype(jnp.float32), axis=0)
    grad_input_norm, gain_one_grad, shift_one_grad = norm_one_back(
        contract_cols(grad_projected, qkv_weight)
    )
    input_grad = (grad_middle + grad_input_norm).astype(jnp.bfloat16)
    row_count = lax.axis_size("dp")
    grad_list = (
        gain_one_grad,
        shift_one_grad,
        qkv_grad,
        qkv_bias_grad,
        proj_grad,
        proj_bias_grad,
        gain_two_grad,
        shift_two_grad,
        fc1_grad,
        fc1_bias_grad,
        fc2_grad,
        fc2_bias_grad,
    )
    packed = jnp.concatenate(
        [(grad_item * factor).reshape(row_count, -1) for grad_item in grad_list], axis=1
    )
    grad_part = lax.psum_scatter(packed, "dp", scatter_dimension=0, tiled=True)
    summed = lax.psum(grad_part, "grp")
    bias_width = fc2_bias.shape[0] // row_count
    summed_bias = summed[0, summed.shape[1] - bias_width :]
    own_index = lax.axis_index("dp")
    weight_list = (
        norm1_gain,
        norm1_bias,
        qkv_weight,
        qkv_bias,
        proj_weight,
        proj_bias,
        norm2_gain,
        norm2_bias,
        fc1_weight,
        fc1_bias,
        fc2_weight,
        fc2_bias,
    )
    current = jnp.concatenate(
        [
            lax.dynamic_slice_in_dim(weight_item.reshape(row_count, -1), own_index, 1, 0).astype(
                jnp.float32
            )
            for weight_item in weight_list
        ],
        axis=1,
    )
    decay = jnp.concatenate(
        [
            jnp.full((1, weight_item.size // row_count), decay_flag, jnp.float32)
            for weight_item, decay_flag in zip(weight_list, decay_flags)
        ],
        axis=1,
    )
    new_first = beta_one * first_moment + (1.0 - beta_one) * summed
    new_second = beta_two * second_moment + (1.0 - beta_two) * summed * summed
    ratio = (
        new_first
        / (1.0 - beta_one**step_count)
        / (jnp.sqrt(new_second / (1.0 - beta_two**step_count)) + adam_eps)
    )
    fresh_low = (current - learn_rate * (ratio + decay_rate * decay * current)).astype(jnp.bfloat16)
    new_weights = lax.all_gather(fresh_low, "dp", axis=0, tiled=True)
    return (block_out, input_grad, summed, new_weights, new_first, new_second, summed_bias)


def solution(mesh):
    in_specs = (
        P(("grp", "dp"), None),
        P(("grp", "dp"), None),
        P(("grp", "dp"), None),
        P(("grp", "dp")),
        P(),
        P(),
        P(),
        P(),
        P(),
        P(),
        P(),
        P(),
        P(),
        P(),
        P(),
        P(),
        P(),
        P("dp", None),
        P("dp", None),
    )
    out_specs = (
        P(("grp", "dp"), None),
        P(("grp", "dp"), None),
        P("dp", None),
        P(),
        P("dp", None),
        P("dp", None),
        P("dp"),
    )
    return jax.shard_map(
        on_device, mesh=mesh, in_specs=in_specs, out_specs=out_specs, check_vma=False
    )
```

profile of v0, /device:TPU:0, one launch (start us, length us, event | category | flops | bytes accessed | tf_op | source)
XLA Modules:
  0.0 1624.3 jit_solution(11156478044281256966)
XLA Ops:
  10.4 6.4 add_convert_fusion
  26.9 12.2 fusion.19
  39.1 11.8 fusion
  54.0 12.7 fusion.44
  69.0 12.4 fusion.20
  81.4 13.4 fusion.1
  97.3 8.5 fusion.45
  114.6 10.8 fusion.63
  125.5 16.4 %convert_reduce_fusion = (f32[3072]{0:T(1024)}, bf16[1024,3072]{1,0:T(8,128)(2,1)S(1)}) fusion(f32[1024,3072]{1,0:T(8,128)} %fusion.63, f32[3072]{0:T(1024)S(1)} %convert_element_type.143, bf16[3072,768]{1,0:T(8,128)(2,1)} %param.34, bf16[1024,768]{0,1:T(8,128)(2,1)S(1)} %copy-done.14, f32[1024]{0:T(1024)S(1)} %fusion.47), kind=kOutput, calls=%fused_computation.28 | convolution fusion | flops 4906546176 | bytes 25194496 | tf_op jit(solution)/shard_map/dot_general | solution.py:38
  141.9 7.3 fusion.73
  149.2 3.5 copy.98
  162.8 21.6 %multiply_reduce_fusion.1 = (f32[12,512]{1,0:T(8,128)S(1)}, f32[12,512,1024]{2,1,0:T(8,128)}) fusion(f32[12,512]{1,0:T(8,128)S(1)} %copy-done.43, f32[12,512,1024]{2,1,0:T(8,128)} %get-tuple-element.68, pred[512,1024]{1,0:T(8,128)(4,1)S(1)} %copy-done.18, bf16[512,12,64]{0,2,1:T(8,128)(2,1)S(1)} %bitcast.95, bf16[1024,12,64]{0,2,1:T(8,128)(2,1)S(1)} %bitcast.81), kind=kOutput, calls=%fused_computation.4 | convolution fusion | flops 836757504 | bytes 53264384 | tf_op jit(solution)/shard_map/qhd,khd->hqk/dot_general | solution.py:168
  184.4 17.7 %multiply_reduce_fusion = (f32[12,512]{1,0:T(8,128)S(1)}, f32[12,512,1024]{2,1,0:T(8,128)}) fusion(f32[12,512]{1,0:T(8,128)S(1)} %log_add_fusion, f32[12,512,1024]{2,1,0:T(8,128)} %get-tuple-element.66, pred[512,1024]{1,0:T(8,128)(4,1)S(1)} %copy-done.20, bf16[512,12,64]{0,2,1:T(8,128)(2,1)} %bitcast.97, bf16[1024,12,64]{0,2,1:T(8,128)(2,1)S(1)} %bitcast.82), kind=kOutput, calls=%fused_computation.1 | convolution fusion | flops 836757504 | bytes 53264384 | tf_op jit(solution)/shard_map/qhd,khd->hqk/dot_general | solution.py:168
  202.1 42.2 %multiply_convert_fusion = (bf16[12,512,1024]{2,1,0:T(8,128)(2,1)}, bf16[12,512,1024]{2,1,0:T(8,128)(2,1)}) fusion(f32[12,512,1024]{2,1,0:T(8,128)} %get-tuple-element.74, f32[12,512]{1,0:T(8,128)S(1)} %get-tuple-element.73, f32[12,512]{1,0:T(8,128)S(1)} %log_add_fusion, f32[12,512,1024]{2,1,0:T(8,128)} %get-tuple-element.66, ...), kind=kLoop, calls=%fused_computation | loop fusion | flops 75497472 | bytes 126976000 | tf_op jit(solution)/shard_map/convert_element_type | solution.py:173
  244.3 9.6 fusion.42
  253.9 8.8 fusion.74
  262.7 13.3 fusion.11
  276.7 6.3 fusion.43
  283.0 5.6 multiply_convert_fusion.3
  288.6 13.0 add_convert_fusion.2
  305.3 5.6 fusion.72
  312.1 42.2 %psum.14 = s32[3]{0:T(128)S(1)} all-reduce(s32[3]{0:T(128)S(1)} %fusion.51), channel_id=1, replica_groups=mesh['grp'=2,'dp'=16] {'grp','dp'}, use_global_device_ids=true, to_apply=%region_19.20 | all-reduce | flops 3 | bytes 24 | tf_op jit(solution)/shard_map/psum | solution.py:82
  357.0 9.0 convolution_multiply_fusion
  368.9 10.7 convolution_multiply_fusion.2
  379.7 10.9 convolution_multiply_fusion.1
  390.7 5.6 reshape.518
  396.3 4.0 copy.99
  407.8 10.7 reshape.520
  418.6 10.6 reshape.521
  429.2 5.6 fusion.32
  437.7 20.7 %dynamic-update-slice.24 = f32[16,442992]{1,0:T(8,128)} dynamic-update-slice(f32[16,442992]{1,0:T(8,128)} %dynamic-update-slice.23, f32[16,110592]{1,0:T(8,128)} %reshape.518, s32[]{} %constant.87, s32[]{} %constant.88) | dynamic-update-slice | bytes 14155780
  459.9 7.6 dynamic-update-slice.26
  471.9 6.5 constant_dynamic-update-slice_fusion
  479.8 27.0 %dynamic-update-slice.32 = f32[16,442992]{1,0:T(8,128)} dynamic-update-slice(f32[16,442992]{1,0:T(8,128)} %dynamic-update-slice.31, f32[16,147456]{1,0:T(8,128)} %reshape.521, s32[]{} %constant.87, s32[]{} %constant.95) | dynamic-update-slice | bytes 18874372
  518.2 5.2 reshape.530
  523.4 5.2 reshape.532
  533.8 8.7 dynamic-update-slice.1
  544.0 3.8 dynamic-update-slice.3
  555.0 8.8 dynamic-update-slice.12
  565.3 3.7 dynamic-update-slice.14
  576.1 667.0 %all-reduce.6.cloned.1.call-done = f32[16,442992]{1,0:T(8,128)} async-done(((f32[16,442992]{1,0:T(8,128)}), f32[16,442992]{1,0:T(8,128)}) %all-reduce.6.cloned.1.call-update) | async-done | bytes 28351504
  1243.1 7.5 constant_dynamic-slice_fusion.11
  1255.6 11.4 dynamic-update-slice.8
  1269.6 11.3 dynamic-update-slice.20
  1282.1 14.6 convert_bitcast_fusion
  1299.5 11.8 add_convert_fusion.3
  1315.2 282.6 %all-gather.3.cloned.1.call-done = bf16[16,1,442992]{2,1,0:T(2,128)(2,1)} async-done(((bf16[1,1,442992]{2,1,0:T(2,128)(2,1)}), bf16[16,1,442992]{2,1,0:T(2,128)(2,1)}) %all-gather.3.cloned.1.call-update) | async-done | bytes 14175760 | tf_op jit(solution)/shard_map/all_gather | solution.py:266
  1597.8 18.5 %copy.107 = bf16[16,1,442992]{2,0,1:T(8,128)(2,1)} copy(bf16[16,1,442992]{2,1,0:T(2,128)(2,1)} %all-gather.3.cloned.1.call-done) | data formatting | bytes 28351488
  (313 shorter events, 116.6 us)
Async XLA Ops:
  7.2 1235.9 %all-reduce.6.cloned.1.call-start = ((), (), s32[]{:S(2)}) async-start(), calls=%async_computation.2 | async-start | bytes 56705024
  9.0 98.3 %copy-start.1 = (bf16[1024,768]{0,1:T(8,128)(2,1)}, bf16[1024,768]{0,1:T(8,128)(2,1)S(1)}, u32[]{:S(2)}) copy-start(bf16[1024,768]{0,1:T(8,128)(2,1)S(1)} %copy.90) | copy-start | bytes 4718596
  22.5 46.6 %copy-start.8 = (bf16[1024,768]{0,1:T(8,128)(2,1)}, bf16[1024,768]{0,1:T(8,128)(2,1)S(1)}, u32[]{:S(2)}) copy-start(bf16[1024,768]{0,1:T(8,128)(2,1)S(1)} %copy.94) | copy-start | bytes 4718596
  26.9 12.2 copy-start.17
  69.0 25.9 %copy-start.12 = (bf16[1024,768]{0,1:T(8,128)(2,1)S(1)}, bf16[1024,768]{0,1:T(8,128)(2,1)}, u32[]{:S(2)}) copy-start(bf16[1024,768]{0,1:T(8,128)(2,1)} %copy.91) | copy-start | bytes 4718596
  81.4 15.8 copy-start
  81.4 15.9 copy-start.19
  97.3 8.5 copy-start.40
  111.1 14.4 copy-start.41
  114.6 10.9 copy-start.60
  114.6 10.9 copy-start.14
  114.6 27.3 %slice-start.3 = ((s8[4718592]{0:T(1024)(128)(4,1)}), s8[4194304]{0:T(1024)(128)(4,1)S(1)}, s32[]{:S(2)}) async-start(s8[4718592]{0:T(1024)(128)(4,1)} %bitcast.76), calls=%async_computation.6 | async-start | bytes 8388608
  125.5 16.4 %slice-start.4 = ((s8[4718592]{0:T(1024)(128)(4,1)}), s8[524288]{0:T(1024)(128)(4,1)S(1)}, s32[]{:S(2)}) async-start(s8[4718592]{0:T(1024)(128)(4,1)} %bitcast.76), calls=%async_computation.7 | async-start | bytes 1048576
  162.0 22.4 %copy-start.30 = (bf16[512,768]{0,1:T(8,128)(2,1)}, bf16[512,768]{0,1:T(8,128)(2,1)S(1)}, u32[]{:S(2)}) copy-start(bf16[512,768]{0,1:T(8,128)(2,1)S(1)} %get-tuple-element.59) | copy-start | bytes 2359300
  162.8 21.7 %copy-start.20 = (pred[512,1024]{1,0:T(8,128)(4,1)S(1)}, pred[512,1024]{1,0:T(8,128)(4,1)}, u32[]{:S(2)}) copy-start(pred[512,1024]{1,0:T(8,128)(4,1)} %get-tuple-element.62) | copy-start | bytes 1572868
  202.1 42.2 %copy-start.9 = (bf16[1024,768]{0,1:T(8,128)(2,1)S(1)}, bf16[1024,768]{0,1:T(8,128)(2,1)}, u32[]{:S(2)}) copy-start(bf16[1024,768]{0,1:T(8,128)(2,1)} %copy-done.8) | copy-start | bytes 4718596
  244.3 9.6 copy-start.24
  253.9 8.8 copy-start.21
  253.9 8.8 copy-start.31
  253.9 22.7 %slice-start = ((s8[12582912]{0:T(1024)(128)(4,1)}), s8[4194304]{0:T(1024)(128)(4,1)S(1)}, s32[]{:S(2)}) async-start(s8[12582912]{0:T(1024)(128)(4,1)} %bitcast.70), calls=%async_computation.3 | async-start | bytes 8388608
  253.9 22.7 %slice-start.1 = ((s8[12582912]{0:T(1024)(128)(4,1)}), s8[4194304]{0:T(1024)(128)(4,1)S(1)}, s32[]{:S(2)}) async-start(s8[12582912]{0:T(1024)(128)(4,1)} %bitcast.70), calls=%async_computation.4 | async-start | bytes 8388608
  262.7 13.3 copy-start.77
  262.7 13.9 slice-start.2
  288.6 13.1 copy-start.28
  288.6 13.1 copy-start.29
  301.8 9.0 copy-start.26
  305.3 50.3 %copy-start.78 = (s32[3]{0:T(128)S(1)}, s32[3]{0:T(128)}, u32[]{:S(2)}) copy-start(s32[3]{0:T(128)} %param.23) | copy-start | bytes 40
  305.3 51.7 %copy-start.2 = (bf16[1024,768]{0,1:T(8,128)(2,1)S(1)}, bf16[1024,768]{0,1:T(8,128)(2,1)}, u32[]{:S(2)}) copy-start(bf16[1024,768]{0,1:T(8,128)(2,1)} %copy-done.1) | copy-start | bytes 4718596
  305.3 51.7 %copy-start.45 = (f32[1024]{0:T(1024)S(1)}, f32[1024]{0:T(1024)}, u32[]{:S(2)}) copy-start(f32[1024]{0:T(1024)} %copy-done.44) | copy-start | bytes 12292
  305.3 51.7 %copy-start.47 = (f32[768]{0:T(1024)S(1)}, f32[768]{0:T(1024)}, u32[]{:S(2)}) copy-start(f32[768]{0:T(1024)} %copy-done.46) | copy-start | bytes 9220
  305.3 51.7 %copy-start.49 = (f32[1024]{0:T(1024)S(1)}, f32[1024]{0:T(1024)}, u32[]{:S(2)}) copy-start(f32[1024]{0:T(1024)} %copy-done.48) | copy-start | bytes 12292
  305.3 51.7 %copy-start.74 = (f32[768]{0:T(1024)S(1)}, f32[768]{0:T(1024)}, u32[]{:S(2)}) copy-start(f32[768]{0:T(1024)} %copy-done.73) | copy-start | bytes 9220
  357.0 9.0 copy-start.34
  357.0 9.0 copy-start.36
  366.0 13.7 slice-start.5
  368.9 10.8 copy-start.16
  368.9 10.8 slice-start.6
  368.9 10.8 slice-start.7
  368.9 10.8 copy-start.61
  407.8 10.7 copy-start.63
  418.6 10.7 copy-start.53
  437.7 22.2 %copy-start.23 = (f32[16,36864]{1,0:T(8,128)S(1)}, f32[16,36864]{1,0:T(8,128)}, u32[]{:S(2)}) copy-start(f32[16,36864]{1,0:T(8,128)} %reshape.519) | copy-start | bytes 7077892
  508.1 774.0 %all-reduce.4.cloned.1.call-start = ((), (), s32[]{:S(2)}) async-start(), calls=%async_computation | async-start | bytes 3544064 | tf_op jit(solution)/shard_map/psum | solution.py:224
  1243.1 10.7 copy-start.57
  1243.1 10.7 copy-start.72
  1250.7 31.4 %copy-start.32 = (f32[1,442992]{1,0:T(1,128)S(1)}, f32[1,442992]{1,0:T(1,128)}, u32[]{:S(2)}) copy-start(f32[1,442992]{1,0:T(1,128)} %param.36) | copy-start | bytes 5315908
  1250.7 347.1 %all-gather.3.cloned.1.call-start = ((), (), s32[]{:S(2)}) async-start(), calls=%async_computation.1 | async-start | bytes 30124544 | tf_op jit(solution)/shard_map/all_gather | solution.py:266
  1315.2 301.2 %copy-start.25 = (f32[1,442992]{1,0:T(1,128)S(1)}, f32[1,442992]{1,0:T(1,128)}, u32[]{:S(2)}) copy-start(f32[1,442992]{1,0:T(1,128)} %all-reduce.4.cloned.1.call-done) | copy-start | bytes 5315908
  (43 other events, 131.1 us)
Sparse Core Ops, SparseCore 0:
  508.2 734.8 all-reduce.5
  1250.8 19.8 all-reduce.3
  1296.9 300.8 all-gather.2
where the time goes:
time: 1640 us; the launch traced here: 1620 us
  waiting for transfers between devices  950 us (58%)
  local copies, waits for them, and re-layouts  272 us (17%)
  matrix products  237 us (14%)
  other arithmetic  106 us (6%)
  blocking collectives  42.2 us (3%)
  between operations  17 us (1%)
    unnamed x4, waiting for transfers between devices  667 us
    all_gather x1, waiting for transfers between devices, on_device(): new_weights = lax.all_gather(fresh_low, 'dp', axis=0, tiled=True)  283 us
    unnamed x215, local copies, waits for them, and re-layouts  188 us
    psum x1, blocking collectives, on_device(): totals = lax.psum(member * images, ('grp', 'dp'))  42.2 us
    convert_element_type x1, other arithmetic, on_device(): grad_scores = (attn_probs * (grad_probs - jnp.sum(attn_probs * grad_probs...  42.2 us
    dot_general x2, matrix products, on_device(): jnp.einsum('qhd,khd->hqk', context_grad_part, value_rows, preferred_eleme...  39.4 us
    dot_general x4, matrix products, contract_rows(): lax.dot_general(first_op, second_op, (((0,), (0,)), ((), ())), preferred_...  33.5 us
  transfers between devices with their start and end apart: 3, of which 2 were waited for; matrix products, arithmetic and copies ran while one was open for 7% of the time, Pallas kernels for 0%

commit v1 on v0

--- a/solution.py
+++ b/solution.py
@@ -263,7 +263,15 @@
         / (jnp.sqrt(new_second / (1.0 - beta_two**step_count)) + adam_eps)
     )
     fresh_low = (current - learn_rate * (ratio + decay_rate * decay * current)).astype(jnp.bfloat16)
-    new_weights = lax.all_gather(fresh_low, "dp", axis=0, tiled=True)
+    ways, here = (lax.axis_size("dp"), lax.axis_index("dp"))
+    grown, reach = (fresh_low, 1)
+    while reach < ways:
+        theirs = lax.ppermute(grown, "dp", [(d, d ^ reach) for d in range(ways)])
+        mine_first = jnp.concatenate([grown, theirs], axis=0)
+        theirs_first = jnp.concatenate([theirs, grown], axis=0)
+        grown = jnp.where(here & reach == 0, mine_first, theirs_first)
+        reach = 2 * reach
+    new_weights = grown
     return (block_out, input_grad, summed, new_weights, new_first, new_second, summed_bias)
 
 

time: 1640 us -> 1840 us (1.12)
  waiting for transfers between devices: 950 us -> 1110 us
  other arithmetic: 106 us -> 163 us
  local copies, waits for them, and re-layouts: 272 us -> 253 us
    ppermute x0 -> x4, waiting for transfers between devices: none -> 438 us  [on_device(): theirs = lax.ppermute(grown, 'dp', [(d, d ^ reach) for d in range(ways)])]
    all_gather x1 -> x0, waiting for transfers between devices: 283 us -> none  [on_device(): new_weights = lax.all_gather(fresh_low, 'dp', axis=0, tiled=True)]
    select_n x0 -> x4, other arithmetic: none -> 57 us  [on_device(): grown = jnp.where(here & reach == 0, mine_first, theirs_first)]
    unnamed x215 -> x212, local copies, waits for them, and re-layouts: 188 us -> 169 us
    unnamed x4 -> x3, waiting for transfers between devices: 667 us -> 667 us
  transfers between devices with their start and end apart: 3 -> 6, of which waited for: 2 -> 5; matrix products, arithmetic and copies ran while one was open for 7% -> 6% of each run, Pallas kernels for 0% -> 0%
where the time goes in v1:
time: 1840 us; the launch traced here: 1820 us
  waiting for transfers between devices  1110 us (60%)
  local copies, waits for them, and re-layouts  253 us (14%)
  matrix products  237 us (13%)
  other arithmetic  163 us (9%)
  blocking collectives  42.4 us (2%)
    unnamed x3, waiting for transfers between devices  667 us
    ppermute x4, waiting for transfers between devices, on_device(): theirs = lax.ppermute(grown, 'dp', [(d, d ^ reach) for d in range(ways)])  438 us
    unnamed x212, local copies, waits for them, and re-layouts  169 us
    select_n x4, other arithmetic, on_device(): grown = jnp.where(here & reach == 0, mine_first, theirs_first)  57 us
    psum x1, blocking collectives, on_device(): totals = lax.psum(member * images, ('grp', 'dp'))  42.4 us
    convert_element_type x1, other arithmetic, on_device(): grad_scores = (attn_probs * (grad_probs - jnp.sum(attn_probs * grad_probs...  42 us
    dot_general x2, matrix products, on_device(): jnp.einsum('qhd,khd->hqk', context_grad_part, value_rows, preferred_eleme...  39.6 us
  transfers between devices with their start and end apart: 6, of which 5 were waited for; matrix products, arithmetic and copies ran while one was open for 6% of the time, Pallas kernels for 0%

profile of v1, /device:TPU:0, one launch (start us, length us, event | category | flops | bytes accessed | tf_op | source)
XLA Modules:
  0.0 1823.2 jit_solution(5088698939352009275)
XLA Ops:
  10.4 6.4 add_convert_fusion
  26.9 12.2 fusion.19
  39.1 11.8 fusion
  54.0 12.7 fusion.44
  69.0 12.2 fusion.20
  81.2 13.4 fusion.1
  97.1 8.5 fusion.45
  114.4 10.8 fusion.63
  125.3 16.5 convert_reduce_fusion
  141.7 7.3 fusion.73
  162.6 21.8 %multiply_reduce_fusion.1 = (f32[12,512]{1,0:T(8,128)S(1)}, f32[12,512,1024]{2,1,0:T(8,128)}) fusion(f32[12,512]{1,0:T(8,128)S(1)} %copy-done.43, f32[12,512,1024]{2,1,0:T(8,128)} %get-tuple-element.61, pred[512,1024]{1,0:T(8,128)(4,1)S(1)} %copy-done.18, bf16[512,12,64]{0,2,1:T(8,128)(2,1)S(1)} %bitcast.89, bf16[1024,12,64]{0,2,1:T(8,128)(2,1)S(1)} %bitcast.75), kind=kOutput, calls=%fused_computation.4 | convolution fusion | flops 836757504 | bytes 53264384 | tf_op jit(solution)/shard_map/qhd,khd->hqk/dot_general | solution.py:168
  184.5 17.7 multiply_reduce_fusion
  202.2 42.0 %multiply_convert_fusion = (bf16[12,512,1024]{2,1,0:T(8,128)(2,1)}, bf16[12,512,1024]{2,1,0:T(8,128)(2,1)}) fusion(f32[12,512,1024]{2,1,0:T(8,128)} %get-tuple-element.67, f32[12,512]{1,0:T(8,128)S(1)} %get-tuple-element.66, f32[12,512]{1,0:T(8,128)S(1)} %log_add_fusion, f32[12,512,1024]{2,1,0:T(8,128)} %get-tuple-element.59, ...), kind=kLoop, calls=%fused_computation | loop fusion | flops 75497472 | bytes 126976000 | tf_op jit(solution)/shard_map/convert_element_type | solution.py:173
  244.1 9.6 fusion.42
  253.8 8.8 fusion.74
  262.5 13.4 fusion.11
  276.5 6.3 fusion.43
  282.8 5.6 multiply_convert_fusion.3
  288.4 13.0 add_convert_fusion.2
  305.1 5.6 fusion.72
  311.9 42.4 %psum.14 = s32[3]{0:T(128)S(1)} all-reduce(s32[3]{0:T(128)S(1)} %fusion.51), channel_id=1, replica_groups=mesh['grp'=2,'dp'=16] {'grp','dp'}, use_global_device_ids=true, to_apply=%region_19.20 | all-reduce | flops 3 | bytes 24 | tf_op jit(solution)/shard_map/psum | solution.py:82
  357.0 9.0 convolution_multiply_fusion
  369.0 10.7 convolution_multiply_fusion.2
  379.8 10.9 convolution_multiply_fusion.1
  390.7 5.6 reshape.518
  407.6 10.7 reshape.520
  418.4 10.6 reshape.521
  429.0 5.6 fusion.32
  437.5 20.7 %dynamic-update-slice.24 = f32[16,442992]{1,0:T(8,128)} dynamic-update-slice(f32[16,442992]{1,0:T(8,128)} %dynamic-update-slice.23, f32[16,110592]{1,0:T(8,128)} %reshape.518, s32[]{} %constant.103, s32[]{} %constant.104) | dynamic-update-slice | bytes 14155780
  459.7 7.6 dynamic-update-slice.26
  471.7 6.5 constant_dynamic-update-slice_fusion
  479.6 27.0 %dynamic-update-slice.32 = f32[16,442992]{1,0:T(8,128)} dynamic-update-slice(f32[16,442992]{1,0:T(8,128)} %dynamic-update-slice.31, f32[16,147456]{1,0:T(8,128)} %reshape.521, s32[]{} %constant.103, s32[]{} %constant.111) | dynamic-update-slice | bytes 18874372
  533.6 8.7 dynamic-update-slice.1
  554.9 8.8 dynamic-update-slice.12
  576.0 667.0 %all-reduce.6.cloned.1.call-done = f32[16,442992]{1,0:T(8,128)} async-done(((f32[16,442992]{1,0:T(8,128)}), f32[16,442992]{1,0:T(8,128)}) %all-reduce.6.cloned.1.call-update) | async-done | bytes 28351504
  1243.0 7.5 constant_dynamic-slice_fusion.11
  1255.0 11.4 dynamic-update-slice.8
  1269.0 11.3 dynamic-update-slice.20
  1281.6 14.7 subtract_convert_fusion
  1297.8 39.0 %collective-permute-done = bf16[1,442992]{1,0:T(2,128)(2,1)} collective-permute-done((bf16[1,442992]{1,0:T(2,128)(2,1)S(1)}, bf16[1,442992]{1,0:T(2,128)(2,1)}, u32[]{:S(2)}, u32[]{:S(2)}) %collective-permute-start) | collective-permute-done | bytes 886016 | tf_op jit(solution)/shard_map/ppermute | solution.py:269
  1336.7 12.0 broadcast_select_fusion
  1350.3 38.1 %collective-permute-done.1 = bf16[2,442992]{1,0:T(2,128)(2,1)} collective-permute-done((bf16[2,442992]{1,0:T(2,128)(2,1)S(1)}, bf16[2,442992]{1,0:T(2,128)(2,1)}, u32[]{:S(2)}, u32[]{:S(2)}) %collective-permute-start.1) | collective-permute-done | bytes 1772000 | tf_op jit(solution)/shard_map/ppermute | solution.py:269
  1388.3 12.5 maximum_select_fusion.2
  1400.9 76.6 %collective-permute-done.2 = bf16[4,442992]{1,0:T(4,128)(2,1)} collective-permute-done((bf16[4,442992]{1,0:T(4,128)(2,1)S(1)}, bf16[4,442992]{1,0:T(4,128)(2,1)}, u32[]{:S(2)}, u32[]{:S(2)}) %collective-permute-start.2) | collective-permute-done | bytes 3543968 | tf_op jit(solution)/shard_map/ppermute | solution.py:269
  1477.5 13.1 maximum_select_fusion.1
  1495.0 12.0 add_convert_fusion.3
  1510.8 284.5 %collective-permute-done.3 = bf16[8,442992]{1,0:T(8,128)(2,1)} collective-permute-done((bf16[8,442992]{1,0:T(8,128)(2,1)}, bf16[8,442992]{1,0:T(8,128)(2,1)}, u32[]{:S(2)}, u32[]{:S(2)}) %collective-permute-start.3) | collective-permute-done | bytes 7087904 | tf_op jit(solution)/shard_map/ppermute | solution.py:269
  1795.3 19.4 %maximum_select_fusion = bf16[16,442992]{1,0:T(8,128)(2,1)} fusion(bf16[8,442992]{1,0:T(8,128)(2,1)} %collective-permute-done.3, bf16[8,442992]{1,0:T(8,128)(2,1)} %maximum_select_fusion.1, pred[]{:T(512)S(6)} %eq.71), kind=kLoop, calls=%fused_computation.18 | loop fusion | flops 63790848 | bytes 28351488 | tf_op jit(solution)/shard_map/jit(_where)/select_n | solution.py:272
  (319 shorter events, 146.1 us)
Async XLA Ops:
  7.2 1235.7 %all-reduce.6.cloned.1.call-start = ((), (), s32[]{:S(2)}) async-start(), calls=%async_computation.1 | async-start | bytes 56705024
  9.0 98.1 %copy-start.1 = (bf16[1024,768]{0,1:T(8,128)(2,1)}, bf16[1024,768]{0,1:T(8,128)(2,1)S(1)}, u32[]{:S(2)}) copy-start(bf16[1024,768]{0,1:T(8,128)(2,1)S(1)} %copy.76) | copy-start | bytes 4718596
  22.5 46.6 %copy-start.8 = (bf16[1024,768]{0,1:T(8,128)(2,1)}, bf16[1024,768]{0,1:T(8,128)(2,1)S(1)}, u32[]{:S(2)}) copy-start(bf16[1024,768]{0,1:T(8,128)(2,1)S(1)} %copy.80) | copy-start | bytes 4718596
  26.9 12.2 copy-start.17
  69.0 25.7 %copy-start.12 = (bf16[1024,768]{0,1:T(8,128)(2,1)S(1)}, bf16[1024,768]{0,1:T(8,128)(2,1)}, u32[]{:S(2)}) copy-start(bf16[1024,768]{0,1:T(8,128)(2,1)} %copy.77) | copy-start | bytes 4718596
  81.2 15.8 copy-start
  81.2 15.9 copy-start.19
  110.9 14.4 copy-start.41
  114.4 10.9 copy-start.60
  114.4 10.9 copy-start.14
  114.4 27.3 %slice-start.3 = ((s8[4718592]{0:T(1024)(128)(4,1)}), s8[4194304]{0:T(1024)(128)(4,1)S(1)}, s32[]{:S(2)}) async-start(s8[4718592]{0:T(1024)(128)(4,1)} %bitcast.71), calls=%async_computation.5 | async-start | bytes 8388608
  125.3 16.5 slice-start.4
  161.8 22.6 %copy-start.31 = (bf16[512,768]{0,1:T(8,128)(2,1)}, bf16[512,768]{0,1:T(8,128)(2,1)S(1)}, u32[]{:S(2)}) copy-start(bf16[512,768]{0,1:T(8,128)(2,1)S(1)} %get-tuple-element.52) | copy-start | bytes 2359300
  162.6 21.9 %copy-start.20 = (pred[512,1024]{1,0:T(8,128)(4,1)S(1)}, pred[512,1024]{1,0:T(8,128)(4,1)}, u32[]{:S(2)}) copy-start(pred[512,1024]{1,0:T(8,128)(4,1)} %get-tuple-element.55) | copy-start | bytes 1572868
  202.2 42.0 %copy-start.9 = (bf16[1024,768]{0,1:T(8,128)(2,1)S(1)}, bf16[1024,768]{0,1:T(8,128)(2,1)}, u32[]{:S(2)}) copy-start(bf16[1024,768]{0,1:T(8,128)(2,1)} %copy-done.8) | copy-start | bytes 4718596
  244.1 9.6 copy-start.24
  253.7 8.8 copy-start.32
  253.7 22.8 %slice-start = ((s8[12582912]{0:T(1024)(128)(4,1)}), s8[4194304]{0:T(1024)(128)(4,1)S(1)}, s32[]{:S(2)}) async-start(s8[12582912]{0:T(1024)(128)(4,1)} %bitcast.65), calls=%async_computation.2 | async-start | bytes 8388608
  253.7 22.8 %slice-start.1 = ((s8[12582912]{0:T(1024)(128)(4,1)}), s8[4194304]{0:T(1024)(128)(4,1)S(1)}, s32[]{:S(2)}) async-start(s8[12582912]{0:T(1024)(128)(4,1)} %bitcast.65), calls=%async_computation.3 | async-start | bytes 8388608
  262.5 13.4 copy-start.76
  262.5 14.0 slice-start.2
  288.4 13.1 copy-start.29
  288.4 13.1 copy-start.30
  301.7 9.0 copy-start.27
  305.1 50.5 %copy-start.77 = (s32[3]{0:T(128)S(1)}, s32[3]{0:T(128)}, u32[]{:S(2)}) copy-start(s32[3]{0:T(128)} %param.23) | copy-start | bytes 40
  305.1 51.9 %copy-start.2 = (bf16[1024,768]{0,1:T(8,128)(2,1)S(1)}, bf16[1024,768]{0,1:T(8,128)(2,1)}, u32[]{:S(2)}) copy-start(bf16[1024,768]{0,1:T(8,128)(2,1)} %copy-done.1) | copy-start | bytes 4718596
  305.1 51.9 %copy-start.45 = (f32[1024]{0:T(1024)S(1)}, f32[1024]{0:T(1024)}, u32[]{:S(2)}) copy-start(f32[1024]{0:T(1024)} %copy-done.44) | copy-start | bytes 12292
  305.1 51.9 %copy-start.47 = (f32[768]{0:T(1024)S(1)}, f32[768]{0:T(1024)}, u32[]{:S(2)}) copy-start(f32[768]{0:T(1024)} %copy-done.46) | copy-start | bytes 9220
  305.1 51.9 %copy-start.49 = (f32[1024]{0:T(1024)S(1)}, f32[1024]{0:T(1024)}, u32[]{:S(2)}) copy-start(f32[1024]{0:T(1024)} %copy-done.48) | copy-start | bytes 12292
  305.1 51.9 %copy-start.73 = (f32[768]{0:T(1024)S(1)}, f32[768]{0:T(1024)}, u32[]{:S(2)}) copy-start(f32[768]{0:T(1024)} %copy-done.72) | copy-start | bytes 9220
  357.0 9.0 copy-start.34
  357.0 9.0 copy-start.36
  366.1 13.7 slice-start.5
  368.9 10.8 copy-start.16
  369.0 10.8 slice-start.6
  369.0 10.8 slice-start.7
  369.0 10.8 copy-start.61
  407.6 10.7 copy-start.62
  418.4 10.7 copy-start.53
  437.5 22.2 %copy-start.23 = (f32[16,36864]{1,0:T(8,128)S(1)}, f32[16,36864]{1,0:T(8,128)}, u32[]{:S(2)}) copy-start(f32[16,36864]{1,0:T(8,128)} %reshape.519) | copy-start | bytes 7077892
  507.9 773.6 %all-reduce.4.cloned.1.call-start = ((), (), s32[]{:S(2)}) async-start(), calls=%async_computation | async-start | bytes 3544064 | tf_op jit(solution)/shard_map/psum | solution.py:224
  1242.9 10.2 copy-start.57
  1243.0 10.3 copy-start.71
  1296.3 40.4 %collective-permute-start = (bf16[1,442992]{1,0:T(2,128)(2,1)S(1)}, bf16[1,442992]{1,0:T(2,128)(2,1)}, u32[]{:S(2)}, u32[]{:S(2)}) collective-permute-start(bf16[1,442992]{1,0:T(2,128)(2,1)S(1)} %get-tuple-element.39), channel_id=1, source_target_pairs={{0,1},{1,0},{2,3},{3,2},{4,5},{5,4},{6,7},{7,6},{8,9},{9,8},{10,11... | collective-permute-start | bytes 2657960 | tf_op jit(solution)/shard_map/ppermute | solution.py:269
  1348.7 39.6 %collective-permute-start.1 = (bf16[2,442992]{1,0:T(2,128)(2,1)S(1)}, bf16[2,442992]{1,0:T(2,128)(2,1)}, u32[]{:S(2)}, u32[]{:S(2)}) collective-permute-start(bf16[2,442992]{1,0:T(2,128)(2,1)S(1)} %broadcast_select_fusion), channel_id=1, source_target_pairs={{0,2},{1,3},{2,0},{3,1},{4,6},{5,7},{6,4},{7,5},{8,10},{9,11},{10,... | collective-permute-start | bytes 5315912 | tf_op jit(solution)/shard_map/ppermute | solution.py:269
  1400.9 76.7 %collective-permute-start.2 = (bf16[4,442992]{1,0:T(4,128)(2,1)S(1)}, bf16[4,442992]{1,0:T(4,128)(2,1)}, u32[]{:S(2)}, u32[]{:S(2)}) collective-permute-start(bf16[4,442992]{1,0:T(4,128)(2,1)S(1)} %maximum_select_fusion.2), channel_id=1, source_target_pairs={{0,4},{1,5},{2,6},{3,7},{4,0},{5,1},{6,2},{7,3},{8,12},{9,13},{10,... | collective-permute-start | bytes 10631816 | tf_op jit(solution)/shard_map/ppermute | solution.py:269
  1490.6 304.6 %collective-permute-start.3 = (bf16[8,442992]{1,0:T(8,128)(2,1)}, bf16[8,442992]{1,0:T(8,128)(2,1)}, u32[]{:S(2)}, u32[]{:S(2)}) collective-permute-start(bf16[8,442992]{1,0:T(8,128)(2,1)} %maximum_select_fusion.1), channel_id=1, source_target_pairs={{0,8},{1,9},{2,10},{3,11},{4,12},{5,13},{6,14},{7,15},{8,0},{9,1},... | collective-permute-start | bytes 21263624 | tf_op jit(solution)/shard_map/ppermute | solution.py:269
  1510.8 303.9 %copy-start.25 = (f32[1,442992]{1,0:T(1,128)S(1)}, f32[1,442992]{1,0:T(1,128)}, u32[]{:S(2)}) copy-start(f32[1,442992]{1,0:T(1,128)} %all-reduce.4.cloned.1.call-done) | copy-start | bytes 5315908
  (45 other events, 148.9 us)
Sparse Core Ops, SparseCore 0:
  508.1 734.8 all-reduce.5
  1250.6 19.8 all-reduce.3
